TPU v7x, 256 devices: a whole 4x4x8 slice. The times are simulated.
256 devices in a mesh: lat: 32 (over y, z_lo, core), tm: 8 (over x, z_hi).
Axes of the slice: x: 4, y: 4, z: 8 (z_hi: 2, z_lo: 4; z = z_hi * 4 + z_lo), core: 2. Of those that a mesh axis runs over, the one named last changes fastest.
Arguments:
- fields: bfloat16 [3, 20, 640, 16, 256], P(None, None, 'lat', None, 'tm'), may hold values from -6 to 6
- vmodes: bfloat16 [20, 16], replicated, may hold values from -1.25 to 1.25
- owner_map: int32 [16], replicated, may hold values from 0 to 15, each once
- hough_table: bfloat16 [16, 15360, 1920], P('tm', 'lat'), may hold values from -0.125 to 0.125
- keep_mask: int32 [16, 15360], P('tm', 'lat'), may hold values 0 or 1
Outputs:
- filtered_fields: bfloat16 [16, 3, 640, 16, 256], P(None, None, 'lat', None, 'tm')
Inputs may be any that keep to these rules, and one draw needn't show every extreme that they name: owner_map is a permutation of 0 to 15; order m uses the rows of hough_table and keep_mask of owner slot owner_map[m].
All inputs are finite; a program needn't handle non-finite values. No bound on the sum of `keep_mask` on one device may be relied on, other than what follows from the above.
Results may differ from a plain program's by a relative error of at most 0.0055.
Values may be sent and summed in bfloat16 or wider, within the bound.
A program may use at most 128 MiB of HBM per device.

v0:
```python
import jax
import jax.numpy as jnp
from jax import lax
from jax.sharding import PartitionSpec as P


def filter_rows(table_rows, keep_rows, columns):
    coefficients = jnp.einsum(
        "knj,kjc->knc", table_rows, columns, preferred_element_type=jnp.float32
    )
    kept = (coefficients * keep_rows.astype(jnp.float32)[:, :, None]).astype(jnp.bfloat16)
    return jnp.einsum("knj,knc->kjc", table_rows, kept, preferred_element_type=jnp.float32)


def copies_path(projected, selection, hough_table, keep_mask):
    outgoing = jnp.einsum(
        "sm,vkamc->skvac",
        selection.astype(jnp.bfloat16),
        projected,
        preferred_element_type=jnp.float32,
    ).astype(jnp.bfloat16)
    incoming = lax.all_to_all(
        lax.all_to_all(outgoing, "lat", split_axis=0, concat_axis=3, tiled=True),
        "tm",
        split_axis=1,
        concat_axis=4,
        tiled=True,
    )
    mode_grp = incoming.shape[1]
    variables = incoming.shape[2]
    lat_count = incoming.shape[3]
    span_cols = incoming.shape[4]
    columns = incoming.reshape(mode_grp, variables * lat_count, span_cols)
    partial_value = filter_rows(hough_table, keep_mask, columns)
    partial_value = partial_value.reshape(1, mode_grp, variables, lat_count, span_cols)
    returned = lax.all_to_all(
        lax.all_to_all(partial_value, "lat", split_axis=3, concat_axis=0, tiled=True),
        "tm",
        split_axis=4,
        concat_axis=1,
        tiled=True,
    )
    combined = jnp.einsum(
        "sm,skvac->kvamc", selection.astype(jnp.float32), returned, precision=lax.Precision.HIGHEST
    )
    return combined.astype(jnp.bfloat16)


def body(fields, vmodes, owner_map, hough_table, keep_mask):
    orders = owner_map.shape[0]
    n_lat = lax.axis_size("lat")
    group_size = n_lat // orders
    projected = jnp.einsum(
        "vlamc,lk->vkamc", fields, vmodes, preferred_element_type=jnp.float32
    ).astype(jnp.bfloat16)
    slot_ids = jnp.arange(n_lat, dtype=jnp.int32)
    selection = owner_map[None, :] == (slot_ids // group_size)[:, None]
    return copies_path(projected, selection, hough_table, keep_mask)


def solution(mesh):
    in_specs = (P(None, None, "lat", None, "tm"), P(), P(), P("tm", "lat", None), P("tm", "lat"))
    out_specs = P(None, None, "lat", None, "tm")
    return jax.shard_map(body, mesh=mesh, in_specs=in_specs, out_specs=out_specs, check_vma=False)
```

profile of v0, /device:TPU:1, one launch (start us, length us, event | category | flops | bytes accessed | tf_op | source)
XLA Modules:
  0.0 538.5 jit_solution(14923107492687805174)
XLA Ops:
  0.7 6.2 %convert_bitcast_fusion.2 = bf16[3,16,20,16,32]{4,1,3,2,0:T(8,128)(2,1)S(1)} fusion(bf16[3,20,20,16,32]{4,3,2,1,0:T(8,128)(2,1)} %param.5, bf16[20,16]{0,1:T(8,128)(2,1)S(1)} %copy-done), kind=kOutput, calls=%fused_computation.5 | convolution fusion | flops 20152320 | bytes 2212480 | tf_op jit(solution)/shard_map/vlamc,lk->vkamc/dot_general | solution.py:53
  6.9 4.9 convert_bitcast_fusion
  11.8 14.3 %copy.27 = bf16[32,16,3,20,32]{4,1,3,2,0:T(8,128)(2,1)} copy(bf16[32,16,3,20,32]{0,4,3,1,2:T(8,128)(2,1)} %convert_bitcast_fusion) | data formatting | bytes 3932160 | tf_op jit(solution)/shard_map/convert_element_type | solution.py:21
  26.0 9.5 %reshape.26 = bf16[32,2,15360]{2,1,0:T(2,128)(2,1)S(1)} reshape(bf16[32,3,20,16,32]{4,3,2,1,0:T(8,128)(2,1)} %bitcast.57) | data formatting | bytes 3932160
  35.6 58.2 %all_to_all.69 = bf16[32,2,15360]{2,1,0:T(2,128)(2,1)} all-to-all(bf16[32,2,15360]{2,1,0:T(2,128)(2,1)S(1)} %reshape.26), channel_id=1, replica_groups=mesh['lat'=32,'tm'=8] {'lat'}, dimensions={0} | all-to-all | bytes 3932160 | tf_op jit(solution)/shard_map/all_to_all | solution.py:23
  93.7 8.8 %reshape.27 = bf16[32,3,20,16,32]{4,3,2,1,0:T(8,128)(2,1)} reshape(bf16[32,2,15360]{2,1,0:T(2,128)(2,1)} %all_to_all.69) | data formatting | bytes 3932160
  102.5 7.7 %bitcast_bitcast_fusion = bf16[1,16,3,32,20,32]{5,1,4,2,3,0:T(8,128)(2,1)} fusion(bf16[32,3,20,16,32]{4,3,2,1,0:T(8,128)(2,1)} %reshape.27), kind=kLoop, calls=%fused_computation.24 | loop fusion | bytes 3932160 | tf_op jit(solution)/shard_map/all_to_all | solution.py:23
  110.2 21.9 %copy.28 = bf16[1,16,3,32,20,32]{4,3,5,2,1,0:T(8,128)(2,1)} copy(bf16[1,16,3,32,20,32]{5,1,4,2,3,0:T(8,128)(2,1)} %bitcast_bitcast_fusion) | data formatting | bytes 3932160 | tf_op jit(solution)/shard_map/all_to_all | solution.py:23
  132.0 22.6 %all_to_all.53 = bf16[1,16,3,640,32]{3,4,2,1,0:T(8,128)(2,1)} reshape(bf16[1,16,3,32,20,32]{4,3,5,2,1,0:T(8,128)(2,1)} %copy.28) | data formatting | bytes 3932160 | tf_op jit(solution)/shard_map/all_to_all | solution.py:23
  154.7 8.3 %all-to-all-start.1 = ((bf16[1,16,3,640,32]{3,4,2,0,1:T(8,128)(2,1)}), bf16[1,16,3,640,32]{3,4,2,0,1:T(8,128)(2,1)S(1)}, u32[]{:S(2)}, u32[]{:S(2)}) async-start(bf16[1,16,3,640,32]{3,4,2,0,1:T(8,128)(2,1)} %bitcast.8), calls=%async_computation.1 | async-start | bytes 3932160 | tf_op jit(solution)/shard_map/all_to_all | solution.py:22
  163.0 47.7 %all-to-all-done.1 = bf16[1,16,3,640,32]{3,4,2,0,1:T(8,128)(2,1)S(1)} async-done(((bf16[1,16,3,640,32]{3,4,2,0,1:T(8,128)(2,1)}), bf16[1,16,3,640,32]{3,4,2,0,1:T(8,128)(2,1)S(1)}, u32[]{:S(2)}, u32[]{:S(2)}) %all-to-all-start.1) | async-done | bytes 1966112 | tf_op jit(solution)/shard_map/all_to_all | solution.py:22
  212.0 2.9 copy.51
  214.8 2.8 reshape.22
  217.7 8.1 %convolution_bitcast_fusion = f32[2,1920,256]{1,2,0:T(8,128)} fusion(bf16[2,480,1920]{2,1,0:T(8,128)(2,1)} %param.8, bf16[2,1920,256]{1,2,0:T(8,128)(2,1)} %reshape.22, f32[2,480]{1,0:T(2,128)S(1)} %convert_element_type.31), kind=kOutput, calls=%fused_computation.6 | convolution fusion | flops 1887928320 | bytes 9588480 | tf_op jit(solution)/shard_map/knj,knc->kjc/dot_general | solution.py:12
  225.8 5.5 %copy.32 = f32[2,1920,256]{2,1,0:T(8,128)} copy(f32[2,1920,256]{1,2,0:T(8,128)} %convolution_bitcast_fusion) | data formatting | bytes 7864320 | tf_op jit(solution)/shard_map/knj,knc->kjc/dot_general | solution.py:12
  231.2 5.1 copy.33
  236.4 95.2 %all_to_all.70 = f32[1,2,3,640,256]{4,1,2,0,3:T(2,128)} all-to-all(f32[1,2,3,640,256]{4,1,2,0,3:T(2,128)S(1)} %copy.33), channel_id=1, replica_groups=mesh['lat'=32,'tm'=8] {'lat'}, dimensions={3} | all-to-all | bytes 7864320 | tf_op jit(solution)/shard_map/all_to_all | solution.py:37
  331.6 21.4 %copy.35 = f32[32,2,3,20,256]{0,1,3,2,4:T(2,128)} copy(f32[32,2,3,20,256]{4,1,2,3,0:T(2,128)} %bitcast.58) | data formatting | bytes 7864320 | tf_op jit(solution)/shard_map/all_to_all | solution.py:37
  353.0 17.8 %reshape.28 = f32[8,1,122880]{2,1,0:T(1,128)} reshape(f32[256,3,20,2,32]{4,3,2,1,0:T(2,128)} %bitcast.54) | data formatting | bytes 7864320
  370.7 94.9 %all_to_all.71 = f32[8,1,122880]{2,1,0:T(1,128)} all-to-all(f32[8,1,122880]{2,1,0:T(1,128)} %reshape.28), channel_id=1, replica_groups=mesh['lat'=32,'tm'=8] {'tm'}, dimensions={0} | all-to-all | bytes 7864320 | tf_op jit(solution)/shard_map/all_to_all | solution.py:36
  466.2 14.1 %reduce = f32[8,122880]{1,0:T(8,128)} reduce(f32[8,1,122880]{2,1,0:T(1,128)} %all_to_all.71, f32[]{:T(128)} %broadcast.32), dimensions={1}, to_apply=%all_to_all.61.reduce_sub_computation | reduce | bytes 7864324 | tf_op jit(solution)/shard_map/all_to_all | solution.py:36
  480.3 23.8 %reshape.29 = f32[256,3,20,2,32]{4,3,2,1,0:T(2,128)} reshape(f32[8,122880]{1,0:T(8,128)} %reduce) | data formatting | bytes 7864320
  504.0 23.2 %copy.43 = f32[32,2,3,20,8,32]{5,0,3,2,1,4:T(8,128)} copy(f32[32,2,3,20,8,32]{0,1,3,2,5,4:T(2,128)} %bitcast.56) | data formatting | bytes 7864320 | tf_op jit(solution)/shard_map/all_to_all | solution.py:36
  527.2 11.0 %convert_bitcast_fusion.1 = bf16[16,3,20,16,32]{4,3,2,1,0:T(8,128)(2,1)} fusion(f32[32,16,3,20,32]{4,0,3,2,1:T(8,128)} %bitcast.55, s32[32]{0:T(128)S(1)} %and_select_fusion, s32[16]{0:T(128)S(1)} %copy-done.4), kind=kOutput, calls=%fused_computation.4 | convolution fusion | flops 189235712 | bytes 4915392 | tf_op jit(solution)/shard_map/sm,skvac->kvamc/dot_general | solution.py:43
  (13 shorter events, 2.5 us)
Async XLA Ops:
  0.0 0.7 copy-start
  0.7 6.2 %copy-start.4 = (s32[16]{0:T(128)S(1)}, s32[16]{0:T(128)}, u32[]{:S(2)}) copy-start(s32[16]{0:T(128)} %param.7) | copy-start | bytes 196
  154.7 8.3 %copy-start.3 = (s32[2,480]{1,0:T(2,128)S(1)}, s32[2,480]{1,0:T(2,128)}, u32[]{:S(2)}) copy-start(s32[2,480]{1,0:T(2,128)} %param.9) | copy-start | bytes 11524
  154.7 56.0 %all-to-all-start.1 = ((bf16[1,16,3,640,32]{3,4,2,0,1:T(8,128)(2,1)}), bf16[1,16,3,640,32]{3,4,2,0,1:T(8,128)(2,1)S(1)}, u32[]{:S(2)}, u32[]{:S(2)}) async-start(bf16[1,16,3,640,32]{3,4,2,0,1:T(8,128)(2,1)} %bitcast.8), calls=%async_computation.1 | async-start | bytes 3932160 | tf_op jit(solution)/shard_map/all_to_all | solution.py:22
  210.7 1.3 copy-start.2
  527.2 11.0 %copy-start.1 = (bf16[20,16]{0,1:T(8,128)(2,1)S(1)}, bf16[20,16]{0,1:T(8,128)(2,1)}, u32[]{:S(2)}) copy-start(bf16[20,16]{0,1:T(8,128)(2,1)} %param.6) | copy-start | bytes 1924
where the time goes:
time: 547 us; the launch traced here: 538 us
  blocking collectives  248 us (45%)
  local copies, waits for them, and re-layouts  190 us (35%)
  waiting for transfers between devices  47.7 us (9%)
  matrix products  30.2 us (6%)
  other arithmetic  14.1 us (3%)
  starting transfers between devices  8.28 us (2%)
    all_to_all x1, blocking collectives, copies_path(): lax.all_to_all(partial_value, 'lat', split_axis=3, concat_axis=0, tiled=T...  95.2 us
    all_to_all x1, blocking collectives, copies_path(): lax.all_to_all(lax.all_to_all(partial_value, 'lat', split_axis=3, concat_...  94.9 us
    unnamed x14, local copies, waits for them, and re-layouts  61.8 us
    all_to_all x1, blocking collectives, copies_path(): lax.all_to_all(outgoing, 'lat', split_axis=0, concat_axis=3, tiled=True)  58.2 us
    all_to_all x3, local copies, waits for them, and re-layouts, copies_path(): lax.all_to_all(outgoing, 'lat', split_axis=0, concat_axis=3, tiled=True)  52.2 us
    all_to_all x1, waiting for transfers between devices, copies_path(): lax.all_to_all(lax.all_to_all(outgoing, 'lat', split_axis=0, concat_axis=...  47.7 us
    all_to_all x2, local copies, waits for them, and re-layouts, copies_path(): lax.all_to_all(lax.all_to_all(partial_value, 'lat', split_axis=3, concat_...  23.7 us
    all_to_all x1, local copies, waits for them, and re-layouts, copies_path(): lax.all_to_all(partial_value, 'lat', split_axis=3, concat_axis=0, tiled=T...  21.4 us
  transfers between devices with their start and end apart: 1, of which 1 were waited for; matrix products, arithmetic and copies ran while one was open for 0% of the time, Pallas kernels for 0%

commit v1 on v0

v1 whole, which is shorter than its diff:
```python
import functools

import jax
import jax.numpy as jnp
from jax import lax
from jax.experimental import pallas as pl
from jax.experimental.pallas import tpu as pltpu
from jax.sharding import PartitionSpec as P

MESH = pl.DeviceIdType.MESH
F32 = jnp.float32
BF16 = jnp.bfloat16


def iota(shape, dim):
    return lax.broadcasted_iota(jnp.int32, shape, dim)


def one_hot(cond):
    return jnp.where(cond, 1.0, 0.0).astype(BF16)


def position():
    lat, tm = lax.axis_index("lat"), lax.axis_index("tm")
    core, z_lo, y = lat % 2, (lat // 2) % 4, lat // 8
    x, z_hi = tm // 2, tm % 2
    return x, y, z_hi * 4 + z_lo, core


def shifted(x, y, z, dx, dy, dz):
    x, y, z = (x + dx) % 4, (y + dy) % 4, (z + dz) % 8
    return y * 4 + z % 4, x * 2 + z // 4


def exchange_kernel(
    fields, vmodes, owner, table, mask,
    arrived,
    f_buf, f_cat, spread, send1, cols, xmat, t_nat, t_ana, t_syn, m_buf, kept, res, send2,
    f_sem, t_sem, m_sem, s1_sem, r1_sem, s2_sem, r2_sem, ready,
):
    x, y, z, core = position()
    slot, tm = y * 4 + z % 4, x * 2 + z // 4
    lat = slot * 2 + core
    other = 1 - core
    partner = (slot * 2 + other, tm)

    barrier = pltpu.get_barrier_semaphore()

    def greet(sem, dx, dy, dz, to_core):
        s, t = shifted(x, y, z, dx, dy, dz)
        pl.semaphore_signal(sem, inc=1, device_id=(s * 2 + to_core, t), device_id_type=MESH)

    loads = [pltpu.make_async_copy(fields.at[v], f_buf.at[v], f_sem.at[v]) for v in range(3)]
    for load in loads:
        load.start()
    for dz in range(8):
        greet(barrier, 0, 0, dz, other)
        if dz:
            greet(barrier, 0, 0, dz, core)
    for s in range(1, 16):
        greet(barrier, s % 4, s // 4, 0, core)
    own_table = pltpu.make_async_copy(table.at[core], t_nat.at[pl.ds(0, 480)], t_sem.at[0])
    own_table.start()
    m_buf[0] = mask[...]

    row_k = (iota((256, 16), 0) % 128) // 16 * 2 + iota((256, 16), 0) // 128
    pick_k = one_hot(row_k == iota((256, 16), 1))
    by_level = lax.dot_general(pick_k, vmodes[...], (((1,), (1,)), ((), ())), preferred_element_type=F32).astype(BF16)
    by_column = jnp.dot(by_level, one_hot(iota((20, 320), 1) // 16 == iota((20, 320), 0)), preferred_element_type=F32)
    owner_lane = jnp.dot(
        owner[...].astype(F32).astype(BF16),
        one_hot(iota((16, 320), 1) % 16 == iota((16, 320), 0)),
        preferred_element_type=F32,
    )
    row_slot = (iota((256, 320), 0) % 16).astype(F32)
    left = jnp.where(row_slot == owner_lane, by_column, 0.0).astype(BF16)

    for v in range(3):
        loads[v].wait()
        for a in range(0, 20, 4):
            pieces = [f_buf[v, :, a + q, :, :].reshape(320, 32) for q in range(4)]
            f_cat[:, pl.ds(v * 640 + a * 32, 128)] = jnp.concatenate(pieces, axis=1)

    pl.semaphore_wait(barrier, 30)
    for dz in range(8):
        greet(ready, 0, 0, dz, other)
        if dz:
            greet(ready, 0, 0, dz, core)

    for half in range(2):
        spread[pl.ds(15, 128, stride=16), :] = jnp.zeros((128, 128), F32)
        for v in range(3):
            part = jnp.dot(left[half * 128:half * 128 + 128], f_cat[:, v * 640:v * 640 + 640], preferred_element_type=F32)
            for a in range(5):
                spread[pl.ds(v * 5 + a, 128, stride=16), :] = part[:, a * 128:a * 128 + 128]
        send1[pl.ds(half * 128, 128)] = spread[...].astype(BF16).reshape(128, 16, 128)
        if half == 0:
            pl.semaphore_wait(ready, 15)
            other_table = pltpu.make_async_remote_copy(
                src_ref=table.at[other], dst_ref=t_nat.at[pl.ds(480, 480)], send_sem=t_sem.at[1], recv_sem=t_sem.at[2],
                device_id=partner, device_id_type=MESH)
            other_mask = pltpu.make_async_remote_copy(
                src_ref=mask, dst_ref=m_buf.at[1], send_sem=m_sem.at[0], recv_sem=m_sem.at[1],
                device_id=partner, device_id_type=MESH)
            other_mask.start()
            other_table.start()

        @pl.loop(0, 128)
        def _(s):
            to_slot, to_tm = shifted(x, y, z, (s // 8) % 4, s // 32, s % 8)
            src = send1.at[half * 128 + to_tm * 16 + to_slot]
            dst = cols.at[tm * 32 + lat]
            away = jnp.logical_or(s > 0, core != half)

            @pl.when(away)
            def _():
                pltpu.make_async_remote_copy(
                    src_ref=src, dst_ref=dst, send_sem=s1_sem, recv_sem=r1_sem,
                    device_id=(to_slot * 2 + half, to_tm), device_id_type=MESH).start()

            @pl.when(jnp.logical_not(away))
            def _():
                pltpu.make_async_copy(src, dst, r1_sem).start()

    own_table.wait()
    other_table.wait()
    other_mask.wait()
    keep = jnp.concatenate(
        [m_buf[0, pl.ds(core, 1), :], m_buf[1, pl.ds(core, 1), :]], axis=1).astype(F32)

    @pl.loop(0, 4)
    def _(g):
        base = pl.multiple_of(g * 128, 128)
        def target(q):
            return g * 32 + (q // 16) % 8 * 20 + q // 128
        ana = jnp.zeros((960, 512), F32)
        syn = jnp.zeros((512, 960), F32)
        for v in range(3):
            window = t_nat[:, pl.ds(pl.multiple_of(v * 640 + base, 128), 256)]
            q, w = iota((256, 512), 1), iota((256, 512), 0)
            r = q % 16 - v * 5
            hot = one_hot((w == target(q) + r * 4) & (r >= 0) & (r < 5))
            ana += jnp.dot(window, hot, preferred_element_type=F32)
            q, w = iota((512, 256), 0), iota((512, 256), 1)
            r = q % 16 - v * 5
            hot = one_hot((w == target(q) + r * 4) & (r >= 0) & (r < 5))
            syn += lax.dot_general(hot, window, (((1,), (1,)), ((), ())), preferred_element_type=F32)
        syn = (syn * keep).astype(BF16)
        ana = ana.astype(BF16)
        for a in range(4):
            t_ana[:, pl.ds(pl.multiple_of(a * 512 + base, 128), 128)] = ana[:, a * 128:a * 128 + 128]
            t_syn[pl.ds(pl.multiple_of(a * 512 + base, 128), 128), :] = syn[a * 128:a * 128 + 128, :]

    pltpu.make_async_copy(cols, cols, r1_sem).wait()
    for a in range(4):
        pieces = [cols[t * 32:t * 32 + 32, :, a * 32:a * 32 + 32].reshape(512, 32) for t in range(8)]
        xmat[a * 512:a * 512 + 512, :] = jnp.concatenate(pieces, axis=1)
    kept[...] = jnp.dot(t_ana[...], xmat[...], preferred_element_type=F32).astype(BF16)
    res[...] = jnp.dot(t_syn[...], kept[...], preferred_element_type=F32).astype(BF16)
    for t in range(8):
        pieces = [res[a * 512:a * 512 + 512, t * 32:t * 32 + 32] for a in range(4)]
        send2[t * 32:t * 32 + 32] = jnp.concatenate(pieces, axis=1).reshape(32, 16, 128)

    for step in range(2):
        @pl.loop(0, 128)
        def _(s):
            to_slot, to_tm = shifted(x, y, z, (s // 8) % 4, s // 32, s % 8)
            to_core = step
            src = send2.at[to_tm * 32 + to_slot * 2 + to_core]
            dst = arrived.at[core * 128 + tm * 16 + slot]
            away = jnp.logical_or(s > 0, core != to_core)

            @pl.when(away)
            def _():
                pltpu.make_async_remote_copy(
                    src_ref=src, dst_ref=dst, send_sem=s2_sem, recv_sem=r2_sem,
                    device_id=(to_slot * 2 + to_core, to_tm), device_id_type=MESH).start()

            @pl.when(jnp.logical_not(away))
            def _():
                pltpu.make_async_copy(src, dst, r2_sem).start()

    sent = pl.ds(0, 255)
    pltpu.make_async_copy(send1.at[sent], send1.at[sent], s1_sem).wait()
    pltpu.make_async_copy(send2.at[sent], send2.at[sent], s2_sem).wait()
    pltpu.make_async_copy(arrived, arrived, r2_sem).wait()


def exchange(fields, vmodes, owner, table, mask):
    vmem, hbm = pl.BlockSpec(memory_space=pltpu.VMEM), pl.BlockSpec(memory_space=pl.ANY)
    dma = pltpu.SemaphoreType.DMA
    return pl.pallas_call(
        exchange_kernel,
        out_shape=jax.ShapeDtypeStruct((256, 16, 128), BF16),
        in_specs=[hbm, vmem, vmem, hbm, vmem],
        out_specs=hbm,
        scratch_shapes=[
            pltpu.VMEM((3, 20, 20, 16, 32), BF16),
            pltpu.VMEM((320, 1920), BF16),
            pltpu.VMEM((2048, 128), F32),
            pltpu.VMEM((256, 16, 128), BF16),
            pltpu.VMEM((256, 16, 128), BF16),
            pltpu.VMEM((2048, 256), BF16),
            pltpu.VMEM((960, 1920), BF16),
            pltpu.VMEM((960, 2048), BF16),
            pltpu.VMEM((2048, 960), BF16),
            pltpu.VMEM((2, 2, 480), jnp.int32),
            pltpu.VMEM((960, 256), BF16),
            pltpu.VMEM((2048, 256), BF16),
            pltpu.VMEM((256, 16, 128), BF16),
            dma((3,)), dma((3,)), dma((2,)), dma, dma, dma, dma,
            pltpu.SemaphoreType.REGULAR,
        ],
        compiler_params=pltpu.CompilerParams(collective_id=0, has_side_effects=True, vmem_limit_bytes=56 * 2**20),
        name="exchange",
    )(fields, vmodes, owner, table, mask)


def lay_out(owner, arrived):
    tiles = arrived.reshape(2, 4, 2, 16, 16, 128)
    def kernel(owner, arrived, out, spread):
        for h in range(4):
            core, t = h % 2, h // 2
            for m in range(16):
                spread[pl.ds(h * 256 + m, 16, stride=16), :] = arrived[core, 0, t, owner[m]].astype(F32)
            for r in range(15):
                rows = spread[h * 256 + r * 16:h * 256 + r * 16 + 16, :].astype(BF16)
                for a in range(4):
                    out[h, r // 5, r % 5 * 4 + a] = rows[:, a * 32:a * 32 + 32]
    return pl.pallas_call(
        kernel,
        grid=(4,),
        out_shape=jax.ShapeDtypeStruct((16, 3, 20, 16, 32), BF16),
        in_specs=[
            pl.BlockSpec(memory_space=pltpu.SMEM),
            pl.BlockSpec((2, 1, 2, 16, 16, 128), lambda g: (0, g, 0, 0, 0, 0)),
        ],
        out_specs=pl.BlockSpec((4, 3, 20, 16, 32), lambda g: (g, 0, 0, 0, 0)),
        scratch_shapes=[pltpu.VMEM((1024, 128), F32)],
        compiler_params=pltpu.CompilerParams(vmem_limit_bytes=24 * 2**20),
        name="lay_out",
    )(owner, tiles)


def body(fields, vmodes, owner_map, hough_table, keep_mask):
    arrived = exchange(fields, vmodes, owner_map.reshape(1, 16), hough_table, keep_mask)
    return lay_out(owner_map, arrived)


def solution(mesh):
    in_specs = (P(None, None, "lat", None, "tm"), P(), P(), P("tm", "lat", None), P("tm", "lat"))
    out_specs = P(None, None, "lat", None, "tm")
    return jax.shard_map(body, mesh=mesh, in_specs=in_specs, out_specs=out_specs, check_vma=False)
```

time: 547 us -> 73.1 us (0.13); the launches traced: 538 us -> 72.9 us
  blocking collectives: 248 us -> 0 us
  local copies, waits for them, and re-layouts: 190 us -> 2.59 us
  Pallas kernels: 0 us -> 70.3 us
  waiting for transfers between devices: 47.7 us -> 0 us
  matrix products: 30.2 us -> 0 us
  other arithmetic: 14.1 us -> 0 us
  starting transfers between devices: 8.28 us -> 0 us
    all_to_all x3 -> x0, blocking collectives: 248 us -> none  [the longest x1 95.2 us: copies_path(): lax.all_to_all(partial_value, 'lat', split_axis=3, concat_axis=0, tiled=T...]
    all_to_all x7 -> x0, local copies, waits for them, and re-layouts: 100 us -> none  [the longest x3 52.2 us: copies_path(): lax.all_to_all(outgoing, 'lat', split_axis=0, concat_axis=3, tiled=True)]
    pallas_call x0 -> x2, Pallas kernels: none -> 70.3 us  [the longest x1 66.2 us: exchange(): pl.pallas_call(exchange_kernel, out_shape=jax.ShapeDtypeStruct((256, 16,...]
    unnamed x14 -> x5, local copies, waits for them, and re-layouts: 61.8 us -> 2.59 us
    all_to_all x1 -> x0, waiting for transfers between devices: 47.7 us -> none  [copies_path(): lax.all_to_all(lax.all_to_all(outgoing, 'lat', split_axis=0, concat_axis=...]
    dot_general x4 -> x0, matrix products: 30.2 us -> none  [the longest x1 11 us: copies_path(): jnp.einsum('sm,skvac->kvamc', selection.astype(jnp.float32), returned, pr...]
    convert_element_type x1 -> x0, local copies, waits for them, and re-layouts: 14.3 us -> none  [copies_path(): outgoing = jnp.einsum('sm,vkamc->skvac', selection.astype(jnp.bfloat16),...]
    all_to_all x1 -> x0, other arithmetic: 14.1 us -> none  [copies_path(): lax.all_to_all(lax.all_to_all(partial_value, 'lat', split_axis=3, concat_...]
  transfers between devices with their start and end apart: 1 -> 0, of which waited for: 1 -> 0; matrix products, arithmetic and copies ran while one was open for 0% -> 0% of each run, Pallas kernels for 0% -> 0%
where the time goes in v1:
time: 73.1 us; the launch traced here: 72.9 us
  Pallas kernels  70.3 us (96%)
  local copies, waits for them, and re-layouts  2.59 us (4%)
    pallas_call x1, Pallas kernels, exchange(): pl.pallas_call(exchange_kernel, out_shape=jax.ShapeDtypeStruct((256, 16,...  66.2 us
    pallas_call x1, Pallas kernels, lay_out(): pl.pallas_call(kernel, grid=(4,), out_shape=jax.ShapeDtypeStruct((16, 3,...  4.07 us
    unnamed x5, local copies, waits for them, and re-layouts  2.59 us

profile of v1, /device:TPU:1, one launch (start us, length us, event | category | flops | bytes accessed | tf_op | source)
XLA Modules:
  0.0 72.9 jit_solution(824765076502616112)
XLA Ops:
  0.0 1.4 %copy.6.vmodes = bf16[20,16]{1,0:T(8,128)(2,1)} copy(bf16[20,16]{0,1:T(8,128)(2,1)} %param.6) | data formatting | bytes 1280 | tf_op args[1]
  1.4 0.0 copy-start.1
  1.4 66.2 %exchange.1 = bf16[256,16,128]{2,1,0:T(8,128)(2,1)} custom-call(bf16[3,20,20,16,32]{4,3,2,1,0:T(8,128)(2,1)} %fields.1, bf16[20,16]{1,0:T(8,128)(2,1)} %copy.6.vmodes, s32[1,16]{1,0:T(1,128)} %bitcast.3, bf16[2,480,1920]{2,1,0:T(8,128)(2,1)} %table.1, s32[2,480]{1,0:T(2,128)} %mask.1), custom_call_target="tpu_custom_call" | custom-call | tf_op jit(solution)/shard_map/exchange/pallas_call | solution.py:192
  67.6 0.0 copy-done.1
  67.6 0.0 copy-start
  67.6 1.2 %copy-done = bf16[256,16,128]{2,1,0:T(8,128)(2,1)S(1)} copy-done((bf16[256,16,128]{2,1,0:T(8,128)(2,1)S(1)}, bf16[256,16,128]{2,1,0:T(8,128)(2,1)}, u32[]{:S(2)}) %copy-start) | copy-done | bytes 1048600
  68.8 4.1 %lay_out.1 = bf16[16,3,20,16,32]{4,3,2,1,0:T(8,128)(2,1)} custom-call(s32[16]{0:T(128)S(1)} %copy-done.1, bf16[2,4,2,16,16,128]{5,4,3,2,1,0:T(8,128)(2,1)S(1)} %bitcast.2), custom_call_target="tpu_custom_call" | custom-call | tf_op jit(solution)/shard_map/lay_out/pallas_call | solution.py:230
Async XLA Ops:
  1.4 66.2 %copy-start.1 = (s32[16]{0:T(128)S(1)}, s32[16]{0:T(128)}, u32[]{:S(2)}) copy-start(s32[16]{0:T(128)} %owner.1) | copy-start | bytes 196
  67.6 1.2 %copy-start = (bf16[256,16,128]{2,1,0:T(8,128)(2,1)S(1)}, bf16[256,16,128]{2,1,0:T(8,128)(2,1)}, u32[]{:S(2)}) copy-start(bf16[256,16,128]{2,1,0:T(8,128)(2,1)} %exchange.1) | copy-start | bytes 3145732

commit v2 on v1

v2 whole, which is shorter than its diff:
```python
import functools

import jax
import jax.numpy as jnp
from jax import lax
from jax.experimental import pallas as pl
from jax.experimental.pallas import tpu as pltpu
from jax.sharding import PartitionSpec as P

MESH = pl.DeviceIdType.MESH
F32 = jnp.float32
BF16 = jnp.bfloat16


def iota(shape, dim):
    return lax.broadcasted_iota(jnp.int32, shape, dim)


def one_hot(cond):
    return jnp.where(cond, 1.0, 0.0).astype(BF16)


def position():
    lat, tm = lax.axis_index("lat"), lax.axis_index("tm")
    core, z_lo, y = lat % 2, (lat // 2) % 4, lat // 8
    x, z_hi = tm // 2, tm % 2
    return x, y, z_hi * 4 + z_lo, core


def shifted(x, y, z, dx, dy, dz):
    x, y, z = (x + dx) % 4, (y + dy) % 4, (z + dz) % 8
    return y * 4 + z % 4, x * 2 + z // 4


def exchange_kernel(
    fields, vmodes, owner, table, mask,
    arrived,
    f_buf, f_cat, spread, send1, cols, xmat, t_nat, t_ana, t_syn, m_buf, coef, kept, send2,
    f_sem, t_sem, m_sem, s1_sem, r1_sem, s2_sem, r2_sem, ready,
):
    x, y, z, core = position()
    slot, tm = y * 4 + z % 4, x * 2 + z // 4
    lat = slot * 2 + core
    other = 1 - core
    partner = (slot * 2 + other, tm)

    barrier = pltpu.get_barrier_semaphore()

    def greet(sem, dx, dy, dz, to_core):
        s, t = shifted(x, y, z, dx, dy, dz)
        pl.semaphore_signal(sem, inc=1, device_id=(s * 2 + to_core, t), device_id_type=MESH)

    loads = [pltpu.make_async_copy(fields.at[v], f_buf.at[v], f_sem.at[v]) for v in range(3)]
    for load in loads:
        load.start()
    for dy in range(1, 4):
        greet(barrier, 0, dy, 0, core)
    greet(barrier, 0, 0, 0, other)

    @pl.loop(1, 32)
    def _(s):
        greet(barrier, s // 8, 0, s % 8, other)
        greet(barrier, s // 8, 0, s % 8, core)

    own_table = pltpu.make_async_copy(table.at[core], t_nat.at[pl.ds(0, 480)], t_sem.at[0])
    own_table.start()
    m_buf[0] = mask[...]

    row_k = (iota((256, 16), 0) % 128) // 16 * 2 + iota((256, 16), 0) // 128
    pick_k = one_hot(row_k == iota((256, 16), 1))
    by_level = jnp.dot(pick_k, vmodes[...], preferred_element_type=F32).astype(BF16)
    by_column = jnp.dot(by_level, one_hot(iota((20, 320), 1) // 16 == iota((20, 320), 0)), preferred_element_type=F32)
    owner_lane = jnp.dot(
        owner[...].astype(F32).astype(BF16),
        one_hot(iota((16, 320), 1) % 16 == iota((16, 320), 0)),
        preferred_element_type=F32,
    )
    row_slot = (iota((256, 320), 0) % 16).astype(F32)
    left = jnp.where(row_slot == owner_lane, by_column, 0.0).astype(BF16)

    for v in range(3):
        loads[v].wait()
        for a in range(0, 20, 4):
            pieces = [f_buf[v, :, a + q, :, :].reshape(320, 32) for q in range(4)]
            f_cat[:, pl.ds(v * 640 + a * 32, 128)] = jnp.concatenate(pieces, axis=1)

    other_table = pltpu.make_async_remote_copy(
        src_ref=table.at[other], dst_ref=t_nat.at[pl.ds(480, 480)], send_sem=t_sem.at[1], recv_sem=t_sem.at[2],
        device_id=partner, device_id_type=MESH)
    other_mask = pltpu.make_async_remote_copy(
        src_ref=mask, dst_ref=m_buf.at[1], send_sem=m_sem.at[0], recv_sem=m_sem.at[1],
        device_id=partner, device_id_type=MESH)
    spread[pl.ds(15, 128, stride=16), :] = jnp.zeros((128, 128), F32)
    my_place = y * 64 + tm * 8 + (z % 4) * 2 + core

    for half in range(2):
        for v in range(3):
            part = jnp.dot(left[half * 128:half * 128 + 128], f_cat[:, v * 640:v * 640 + 640], preferred_element_type=F32)
            for a in range(5):
                spread[pl.ds(v * 5 + a, 128, stride=16), :] = part[:, a * 128:a * 128 + 128]
        send1[pl.ds(half * 128, 128)] = spread[...].astype(BF16).reshape(128, 16, 128)
        if half == 0:
            pl.semaphore_wait(barrier, 66)
            for dy in range(1, 4):
                greet(ready, 0, dy, 0, core)
            other_mask.start()
            other_table.start()
        stay = send1.at[half * 128 + tm * 16 + slot], cols.at[my_place]

        @pl.when(core == half)
        def _():
            pltpu.make_async_copy(*stay, r1_sem.at[0]).start()

        @pl.when(core != half)
        def _():
            pltpu.make_async_remote_copy(
                *stay, send_sem=s1_sem, recv_sem=r1_sem.at[0], device_id=partner, device_id_type=MESH).start()

        for dy in range(4):
            if half == 0 and dy == 1:
                pl.semaphore_wait(ready, 3)

            @pl.loop(0 if dy else 1, 32)
            def _(s):
                to_slot, to_tm = shifted(x, y, z, s // 8, dy, s % 8)
                pltpu.make_async_remote_copy(
                    src_ref=send1.at[half * 128 + to_tm * 16 + to_slot], dst_ref=cols.at[my_place],
                    send_sem=s1_sem, recv_sem=r1_sem.at[dy],
                    device_id=(to_slot * 2 + half, to_tm), device_id_type=MESH).start()

    own_table.wait()
    other_table.wait()
    other_mask.wait()
    keep = jnp.concatenate(
        [m_buf[0, pl.ds(core, 1), :], m_buf[1, pl.ds(core, 1), :]], axis=1).astype(F32)

    @pl.loop(0, 4)
    def _(g):
        base = pl.multiple_of(g * 128, 128)
        def target(q):
            return g * 32 + (q // 16) % 8 * 20 + q // 128
        ana = jnp.zeros((960, 512), F32)
        syn = jnp.zeros((512, 960), F32)
        for v in range(3):
            window = t_nat[:, pl.ds(pl.multiple_of(v * 640 + base, 128), 256)]
            q, w = iota((256, 512), 1), iota((256, 512), 0)
            r = q % 16 - v * 5
            hot = one_hot((w == target(q) + r * 4) & (r >= 0) & (r < 5))
            ana += jnp.dot(window, hot, preferred_element_type=F32)
            q, w = iota((512, 256), 0), iota((512, 256), 1)
            r = q % 16 - v * 5
            hot = one_hot((w == target(q) + r * 4) & (r >= 0) & (r < 5))
            syn += lax.dot_general(hot, window, (((1,), (1,)), ((), ())), preferred_element_type=F32)
        part = pl.ds(pl.multiple_of(g * 512, 512), 512)
        t_syn[part, :] = (syn * keep).astype(BF16)
        t_ana[:, part] = ana.astype(BF16)

    for dy in range(4):
        g = (y + 4 - dy) % 4
        landed = cols.at[pl.ds(g * 64, 64)]
        pltpu.make_async_copy(landed, landed, r1_sem.at[dy]).wait()
        for a in range(4):
            pieces = [cols[pl.ds(g * 64 + t * 8, 8), :, a * 32:a * 32 + 32].reshape(128, 32) for t in range(8)]
            xmat[a * 128:a * 128 + 128, :] = jnp.concatenate(pieces, axis=1)
        add = jnp.dot(t_ana[:, pl.ds(pl.multiple_of(g * 512, 512), 512)], xmat[...], preferred_element_type=F32)
        if dy == 0:
            coef[...] = add
        elif dy < 3:
            coef[...] += add
        else:
            kept[...] = (coef[...] + add).astype(BF16)

    for dy in range(4):
        g = (y + dy) % 4
        back = jnp.dot(t_syn[pl.ds(pl.multiple_of(g * 512, 512), 512), :], kept[...], preferred_element_type=F32).astype(BF16)
        for t in range(8):
            pieces = [back[a * 128:a * 128 + 128, t * 32:t * 32 + 32] for a in range(4)]
            send2[pl.ds(g * 64 + t * 8, 8)] = jnp.concatenate(pieces, axis=1).reshape(8, 16, 128)
        home = arrived.at[core * 128 + tm * 16 + slot]
        if dy == 0:
            pltpu.make_async_copy(send2.at[my_place], home, r2_sem).start()
            pltpu.make_async_remote_copy(
                send2.at[y * 64 + tm * 8 + (z % 4) * 2 + other], home,
                send_sem=s2_sem, recv_sem=r2_sem, device_id=partner, device_id_type=MESH).start()

        @pl.loop(0 if dy else 1, 32)
        def _(s):
            to_slot, to_tm = shifted(x, y, z, s // 8, dy, s % 8)
            for to_core in range(2):
                pltpu.make_async_remote_copy(
                    src_ref=send2.at[g * 64 + to_tm * 8 + to_slot % 4 * 2 + to_core], dst_ref=home,
                    send_sem=s2_sem, recv_sem=r2_sem,
                    device_id=(to_slot * 2 + to_core, to_tm), device_id_type=MESH).start()

    sent = pl.ds(0, 255)
    pltpu.make_async_copy(send1.at[sent], send1.at[sent], s1_sem).wait()
    pltpu.make_async_copy(send2.at[sent], send2.at[sent], s2_sem).wait()
    pltpu.make_async_copy(arrived, arrived, r2_sem).wait()


def exchange(fields, vmodes, owner, table, mask):
    vmem, hbm = pl.BlockSpec(memory_space=pltpu.VMEM), pl.BlockSpec(memory_space=pl.ANY)
    dma = pltpu.SemaphoreType.DMA
    return pl.pallas_call(
        exchange_kernel,
        out_shape=jax.ShapeDtypeStruct((256, 16, 128), BF16),
        in_specs=[hbm, vmem, vmem, hbm, vmem],
        out_specs=hbm,
        scratch_shapes=[
            pltpu.VMEM((3, 20, 20, 16, 32), BF16),
            pltpu.VMEM((320, 1920), BF16),
            pltpu.VMEM((2048, 128), F32),
            pltpu.VMEM((256, 16, 128), BF16),
            pltpu.VMEM((256, 16, 128), BF16),
            pltpu.VMEM((512, 256), BF16),
            pltpu.VMEM((960, 1920), BF16),
            pltpu.VMEM((960, 2048), BF16),
            pltpu.VMEM((2048, 960), BF16),
            pltpu.VMEM((2, 2, 480), jnp.int32),
            pltpu.VMEM((960, 256), F32),
            pltpu.VMEM((960, 256), BF16),
            pltpu.VMEM((256, 16, 128), BF16),
            dma((3,)), dma((3,)), dma((2,)), dma, dma((4,)), dma, dma,
            pltpu.SemaphoreType.REGULAR,
        ],
        compiler_params=pltpu.CompilerParams(collective_id=0, has_side_effects=True, vmem_limit_bytes=56 * 2**20),
        name="exchange",
    )(fields, vmodes, owner, table, mask)


def layout_kernel(owner, arrived, out, order):
    @pl.when(pl.program_id(0) == 0)
    def _():
        mine = iota((256, 16), 0) % 16 == iota((256, 16), 1)
        slot = jnp.sum(jnp.where(mine, owner[...].astype(F32), 0.0), axis=1, keepdims=True).astype(jnp.int32)
        row, column = iota((256, 256), 0), iota((256, 256), 1)
        order[...] = one_hot((column // 16 == slot) & (column % 16 == row // 16))

    tiles = [arrived[h % 2, 0, h // 2].reshape(256, 128) for h in range(4)]
    rows = jnp.dot(order[...], jnp.concatenate(tiles, axis=1), preferred_element_type=F32).astype(BF16)
    for h in range(4):
        for r in range(15):
            for a in range(4):
                out[h, r // 5, r % 5 * 4 + a] = rows[r * 16:r * 16 + 16, h * 128 + a * 32:h * 128 + a * 32 + 32]


def lay_out(owner, arrived):
    return pl.pallas_call(
        layout_kernel,
        grid=(4,),
        out_shape=jax.ShapeDtypeStruct((16, 3, 20, 16, 32), BF16),
        in_specs=[
            pl.BlockSpec(memory_space=pltpu.VMEM),
            pl.BlockSpec((2, 1, 2, 16, 16, 128), lambda g: (0, g, 0, 0, 0, 0)),
        ],
        out_specs=pl.BlockSpec((4, 3, 20, 16, 32), lambda g: (g, 0, 0, 0, 0)),
        scratch_shapes=[pltpu.VMEM((256, 256), BF16)],
        compiler_params=pltpu.CompilerParams(vmem_limit_bytes=60 * 2**20),
        name="lay_out",
    )(owner, arrived.reshape(2, 4, 2, 16, 16, 128))


def body(fields, vmodes, owner_map, hough_table, keep_mask):
    owner = owner_map.reshape(1, 16)
    arrived = exchange(fields, vmodes.T, owner, hough_table, keep_mask)
    return lay_out(owner, arrived)


def solution(mesh):
    in_specs = (P(None, None, "lat", None, "tm"), P(), P(), P("tm", "lat", None), P("tm", "lat"))
    out_specs = P(None, None, "lat", None, "tm")
    return jax.shard_map(body, mesh=mesh, in_specs=in_specs, out_specs=out_specs, check_vma=False)
```

time: 73.1 us -> 66.3 us (0.907)
  Pallas kernels: 70.3 us -> 66.2 us
  local copies, waits for them, and re-layouts: 2.59 us -> 0 us
    pallas_call x1, Pallas kernels: 66.2 us -> 61 us  [exchange(): pl.pallas_call(exchange_kernel, out_shape=jax.ShapeDtypeStruct((256, 16,...]
    unnamed x5 -> x0, local copies, waits for them, and re-layouts: 2.59 us -> none
    pallas_call x1, Pallas kernels: 4.07 us -> 5.18 us  [lay_out(): pl.pallas_call(layout_kernel, grid=(4,), out_shape=jax.ShapeDtypeStruct((...]
where the time goes in v2:
time: 66.3 us; the launch traced here: 66.2 us
  Pallas kernels  66.2 us (100%)
    pallas_call x1, Pallas kernels, exchange(): pl.pallas_call(exchange_kernel, out_shape=jax.ShapeDtypeStruct((256, 16,...  61 us
    pallas_call x1, Pallas kernels, lay_out(): pl.pallas_call(layout_kernel, grid=(4,), out_shape=jax.ShapeDtypeStruct((...  5.18 us

profile of v2, /device:TPU:1, one launch (start us, length us, event | category | flops | bytes accessed | tf_op | source)
XLA Modules:
  0.0 66.2 jit_solution(9752539540674433446)
XLA Ops:
  0.0 61.0 %exchange.1 = bf16[256,16,128]{2,1,0:T(8,128)(2,1)} custom-call(bf16[3,20,20,16,32]{4,3,2,1,0:T(8,128)(2,1)} %fields.1, bf16[16,20]{1,0:T(8,128)(2,1)} %bitcast.4, s32[1,16]{1,0:T(1,128)} %bitcast.5, bf16[2,480,1920]{2,1,0:T(8,128)(2,1)} %table.1, s32[2,480]{1,0:T(2,128)} %mask.1), custom_call_target="tpu_custom_call" | custom-call | tf_op jit(solution)/shard_map/exchange/pallas_call | solution.py:204
  61.0 5.2 %lay_out.1 = bf16[16,3,20,16,32]{4,3,2,1,0:T(8,128)(2,1)} custom-call(s32[1,16]{1,0:T(1,128)} %bitcast.6, bf16[2,4,2,16,16,128]{5,4,3,2,1,0:T(8,128)(2,1)} %bitcast.3), custom_call_target="tpu_custom_call" | custom-call | tf_op jit(solution)/shard_map/lay_out/pallas_call | solution.py:248

commit v3 on v2

--- a/solution.py
+++ b/solution.py
@@ -34,9 +34,9 @@
 
 def exchange_kernel(
     fields, vmodes, owner, table, mask,
-    arrived,
-    f_buf, f_cat, spread, send1, cols, xmat, t_nat, t_ana, t_syn, m_buf, coef, kept, send2,
-    f_sem, t_sem, m_sem, s1_sem, r1_sem, s2_sem, r2_sem, ready,
+    arrived, order_out,
+    order, f_buf, f_cat, spread, send1, cols, xmat, t_nat, t_ana, t_syn, m_buf, coef, kept, send2,
+    o_sem, f_sem, t_sem, m_sem, s1_sem, r1_sem, s2_sem, r2_sem, ready,
 ):
     x, y, z, core = position()
     slot, tm = y * 4 + z % 4, x * 2 + z // 4
@@ -62,8 +62,6 @@
         greet(barrier, s // 8, 0, s % 8, other)
         greet(barrier, s // 8, 0, s % 8, core)
 
-    own_table = pltpu.make_async_copy(table.at[core], t_nat.at[pl.ds(0, 480)], t_sem.at[0])
-    own_table.start()
     m_buf[0] = mask[...]
 
     row_k = (iota((256, 16), 0) % 128) // 16 * 2 + iota((256, 16), 0) // 128
@@ -88,8 +86,9 @@
         src_ref=table.at[other], dst_ref=t_nat.at[pl.ds(480, 480)], send_sem=t_sem.at[1], recv_sem=t_sem.at[2],
         device_id=partner, device_id_type=MESH)
     other_mask = pltpu.make_async_remote_copy(
-        src_ref=mask, dst_ref=m_buf.at[1], send_sem=m_sem.at[0], recv_sem=m_sem.at[1],
+        src_ref=m_buf.at[0], dst_ref=m_buf.at[1], send_sem=m_sem.at[0], recv_sem=m_sem.at[1],
         device_id=partner, device_id_type=MESH)
+    own_table = pltpu.make_async_copy(table.at[core], t_nat.at[pl.ds(0, 480)], t_sem.at[0])
     spread[pl.ds(15, 128, stride=16), :] = jnp.zeros((128, 128), F32)
     my_place = y * 64 + tm * 8 + (z % 4) * 2 + core
 
@@ -105,6 +104,7 @@
                 greet(ready, 0, dy, 0, core)
             other_mask.start()
             other_table.start()
+            own_table.start()
         stay = send1.at[half * 128 + tm * 16 + slot], cols.at[my_place]
 
         @pl.when(core == half)
@@ -127,6 +127,13 @@
                     src_ref=send1.at[half * 128 + to_tm * 16 + to_slot], dst_ref=cols.at[my_place],
                     send_sem=s1_sem, recv_sem=r1_sem.at[dy],
                     device_id=(to_slot * 2 + half, to_tm), device_id_type=MESH).start()
+
+    mine = iota((256, 16), 0) % 16 == iota((256, 16), 1)
+    from_slot = jnp.sum(jnp.where(mine, owner[...].astype(F32), 0.0), axis=1, keepdims=True)
+    row, column = iota((256, 256), 0), iota((256, 256), 1)
+    order[...] = one_hot(((column // 16).astype(F32) == from_slot) & (column % 16 == row // 16))
+    give_order = pltpu.make_async_copy(order, order_out, o_sem)
+    give_order.start()
 
     own_table.wait()
     other_table.wait()
@@ -192,6 +199,7 @@
                     send_sem=s2_sem, recv_sem=r2_sem,
                     device_id=(to_slot * 2 + to_core, to_tm), device_id_type=MESH).start()
 
+    give_order.wait()
     sent = pl.ds(0, 255)
     pltpu.make_async_copy(send1.at[sent], send1.at[sent], s1_sem).wait()
     pltpu.make_async_copy(send2.at[sent], send2.at[sent], s2_sem).wait()
@@ -203,10 +211,11 @@
     dma = pltpu.SemaphoreType.DMA
     return pl.pallas_call(
         exchange_kernel,
-        out_shape=jax.ShapeDtypeStruct((256, 16, 128), BF16),
+        out_shape=[jax.ShapeDtypeStruct((256, 16, 128), BF16), jax.ShapeDtypeStruct((256, 256), BF16)],
         in_specs=[hbm, vmem, vmem, hbm, vmem],
-        out_specs=hbm,
+        out_specs=[hbm, hbm],
         scratch_shapes=[
+            pltpu.VMEM((256, 256), BF16),
             pltpu.VMEM((3, 20, 20, 16, 32), BF16),
             pltpu.VMEM((320, 1920), BF16),
             pltpu.VMEM((2048, 128), F32),
@@ -220,50 +229,48 @@
             pltpu.VMEM((960, 256), F32),
             pltpu.VMEM((960, 256), BF16),
             pltpu.VMEM((256, 16, 128), BF16),
-            dma((3,)), dma((3,)), dma((2,)), dma, dma((4,)), dma, dma,
+            dma, dma((3,)), dma((3,)), dma((2,)), dma, dma((4,)), dma, dma,
             pltpu.SemaphoreType.REGULAR,
         ],
-        compiler_params=pltpu.CompilerParams(collective_id=0, has_side_effects=True, vmem_limit_bytes=56 * 2**20),
+        compiler_params=pltpu.CompilerParams(collective_id=0, has_side_effects=True, vmem_limit_bytes=50 * 2**20),
         name="exchange",
     )(fields, vmodes, owner, table, mask)
 
 
-def layout_kernel(owner, arrived, out, order):
-    @pl.when(pl.program_id(0) == 0)
-    def _():
-        mine = iota((256, 16), 0) % 16 == iota((256, 16), 1)
-        slot = jnp.sum(jnp.where(mine, owner[...].astype(F32), 0.0), axis=1, keepdims=True).astype(jnp.int32)
-        row, column = iota((256, 256), 0), iota((256, 256), 1)
-        order[...] = one_hot((column // 16 == slot) & (column % 16 == row // 16))
-
-    tiles = [arrived[h % 2, 0, h // 2].reshape(256, 128) for h in range(4)]
-    rows = jnp.dot(order[...], jnp.concatenate(tiles, axis=1), preferred_element_type=F32).astype(BF16)
-    for h in range(4):
-        for r in range(15):
+def layout_kernel(order, arrived, out, laid, sem):
+    copies = []
+    for t in range(8):
+        tiles = [arrived[core, t].reshape(256, 128) for core in range(2)]
+        rows = jnp.dot(order[...], jnp.concatenate(tiles, axis=1), preferred_element_type=F32)
+        for core in range(2):
             for a in range(4):
-                out[h, r // 5, r % 5 * 4 + a] = rows[r * 16:r * 16 + 16, h * 128 + a * 32:h * 128 + a * 32 + 32]
-
-
-def lay_out(owner, arrived):
+                part = rows[:, core * 128:core * 128 + 128]
+                part = (pltpu.roll(part, 128 - a * 32, 1) if a else part).astype(BF16)
+                for r in range(15):
+                    laid[t * 2 + core, r // 5, r % 5 * 4 + a] = part[r * 16:r * 16 + 16, 0:32]
+        span = pl.ds(t * 2, 2)
+        copies.append(pltpu.make_async_copy(laid.at[span], out.at[span], sem.at[t]))
+        copies[-1].start()
+    for copy in copies:
+        copy.wait()
+
+
+def lay_out(order, arrived):
+    vmem = pl.BlockSpec(memory_space=pltpu.VMEM)
     return pl.pallas_call(
         layout_kernel,
-        grid=(4,),
         out_shape=jax.ShapeDtypeStruct((16, 3, 20, 16, 32), BF16),
-        in_specs=[
-            pl.BlockSpec(memory_space=pltpu.VMEM),
-            pl.BlockSpec((2, 1, 2, 16, 16, 128), lambda g: (0, g, 0, 0, 0, 0)),
-        ],
-        out_specs=pl.BlockSpec((4, 3, 20, 16, 32), lambda g: (g, 0, 0, 0, 0)),
-        scratch_shapes=[pltpu.VMEM((256, 256), BF16)],
-        compiler_params=pltpu.CompilerParams(vmem_limit_bytes=60 * 2**20),
+        in_specs=[vmem, vmem],
+        out_specs=pl.BlockSpec(memory_space=pl.ANY),
+        scratch_shapes=[pltpu.VMEM((16, 3, 20, 16, 32), BF16), pltpu.SemaphoreType.DMA((8,))],
+        compiler_params=pltpu.CompilerParams(vmem_limit_bytes=16 * 2**20),
         name="lay_out",
-    )(owner, arrived.reshape(2, 4, 2, 16, 16, 128))
+    )(order, arrived.reshape(2, 8, 16, 16, 128))
 
 
 def body(fields, vmodes, owner_map, hough_table, keep_mask):
-    owner = owner_map.reshape(1, 16)
-    arrived = exchange(fields, vmodes.T, owner, hough_table, keep_mask)
-    return lay_out(owner, arrived)
+    arrived, order = exchange(fields, vmodes.T, owner_map.reshape(1, 16), hough_table, keep_mask)
+    return lay_out(order, arrived)
 
 
 def solution(mesh):

time: 66.3 us -> 64.8 us (0.977)
  Pallas kernels: 66.2 us -> 62.6 us
  local copies, waits for them, and re-layouts: 0 us -> 2.03 us
    pallas_call x2, Pallas kernels: 66.2 us -> 62.6 us  [the longest x1 60.2 us: exchange(): pl.pallas_call(exchange_kernel, out_shape=[jax.ShapeDtypeStruct((256, 16,...]
    unnamed x0 -> x6, local copies, waits for them, and re-layouts: none -> 2.03 us
where the time goes in v3:
time: 64.8 us; the launch traced here: 64.7 us
  Pallas kernels  62.6 us (97%)
  local copies, waits for them, and re-layouts  2.03 us (3%)
    pallas_call x1, Pallas kernels, exchange(): pl.pallas_call(exchange_kernel, out_shape=[jax.ShapeDtypeStruct((256, 16,...  60.2 us
    pallas_call x1, Pallas kernels, lay_out(): pl.pallas_call(layout_kernel, out_shape=jax.ShapeDtypeStruct((16, 3, 20,...  2.42 us
    unnamed x6, local copies, waits for them, and re-layouts  2.03 us

profile of v3, /device:TPU:1, one launch (start us, length us, event | category | flops | bytes accessed | tf_op | source)
XLA Modules:
  0.0 64.7 jit_solution(8546201534605773663)
XLA Ops:
  0.0 0.0 copy-start
  0.0 0.7 %copy-done = bf16[20,16]{0,1:T(8,128)(2,1)S(1)} copy-done((bf16[20,16]{0,1:T(8,128)(2,1)S(1)}, bf16[20,16]{0,1:T(8,128)(2,1)}, u32[]{:S(2)}) %copy-start) | copy-done | bytes 664
  0.7 0.0 copy-start.1
  0.7 0.7 %copy-done.1 = s32[2,480]{1,0:T(2,128)S(1)} copy-done((s32[2,480]{1,0:T(2,128)S(1)}, s32[2,480]{1,0:T(2,128)}, u32[]{:S(2)}) %copy-start.1) | copy-done | bytes 3864
  1.4 0.0 copy-start.2
  1.4 0.7 %copy-done.2 = s32[16]{0:T(128)S(1)} copy-done((s32[16]{0:T(128)S(1)}, s32[16]{0:T(128)}, u32[]{:S(2)}) %copy-start.2) | copy-done | bytes 88
  2.0 60.2 %exchange.1 = (bf16[256,16,128]{2,1,0:T(8,128)(2,1)S(1)}, bf16[256,256]{1,0:T(8,128)(2,1)S(1)}) custom-call(bf16[3,20,20,16,32]{4,3,2,1,0:T(8,128)(2,1)} %fields.1, bf16[16,20]{1,0:T(8,128)(2,1)S(1)} %bitcast.4, s32[1,16]{1,0:T(1,128)S(1)} %bitcast.5, bf16[2,480,1920]{2,1,0:T(8,128)(2,1)} %table.1, s32[2,480]{1,0:T(2,128)S(1)} %copy-done.1), custom_call_target="tpu_custom_call" | custom-call | tf_op jit(solution)/shard_map/exchange/pallas_call | solution.py:212
  62.2 2.4 %lay_out.1 = bf16[16,3,20,16,32]{4,3,2,1,0:T(8,128)(2,1)} custom-call(bf16[256,256]{1,0:T(8,128)(2,1)S(1)} %get-tuple-element.7.order, bf16[2,8,16,16,128]{4,3,2,1,0:T(8,128)(2,1)S(1)} %bitcast.3), custom_call_target="tpu_custom_call" | custom-call | tf_op jit(solution)/shard_map/lay_out/pallas_call | solution.py:260
Async XLA Ops:
  0.0 0.7 %copy-start = (bf16[20,16]{0,1:T(8,128)(2,1)S(1)}, bf16[20,16]{0,1:T(8,128)(2,1)}, u32[]{:S(2)}) copy-start(bf16[20,16]{0,1:T(8,128)(2,1)} %param.6) | copy-start | bytes 1924
  0.7 0.7 %copy-start.1 = (s32[2,480]{1,0:T(2,128)S(1)}, s32[2,480]{1,0:T(2,128)}, u32[]{:S(2)}) copy-start(s32[2,480]{1,0:T(2,128)} %mask.1) | copy-start | bytes 11524
  1.4 0.7 %copy-start.2 = (s32[16]{0:T(128)S(1)}, s32[16]{0:T(128)}, u32[]{:S(2)}) copy-start(s32[16]{0:T(128)} %param.7) | copy-start | bytes 196

commit v4 on v3

--- a/solution.py
+++ b/solution.py
@@ -35,8 +35,8 @@
 def exchange_kernel(
     fields, vmodes, owner, table, mask,
     arrived, order_out,
-    order, f_buf, f_cat, spread, send1, cols, xmat, t_nat, t_ana, t_syn, m_buf, coef, kept, send2,
-    o_sem, f_sem, t_sem, m_sem, s1_sem, r1_sem, s2_sem, r2_sem, ready,
+    v_buf, o_buf, order, f_buf, f_cat, spread, send1, cols, xmat, t_nat, t_ana, t_syn, m_buf, coef, kept, send2,
+    i_sem, f_sem, t_sem, m_sem, s1_sem, r1_sem, s2_sem, r2_sem, ready,
 ):
     x, y, z, core = position()
     slot, tm = y * 4 + z % 4, x * 2 + z // 4
@@ -51,7 +51,11 @@
         pl.semaphore_signal(sem, inc=1, device_id=(s * 2 + to_core, t), device_id_type=MESH)
 
     loads = [pltpu.make_async_copy(fields.at[v], f_buf.at[v], f_sem.at[v]) for v in range(3)]
-    for load in loads:
+    small = [
+        pltpu.make_async_copy(src, dst, i_sem.at[i])
+        for i, (src, dst) in enumerate(((vmodes, v_buf), (owner, o_buf), (mask, m_buf.at[0])))
+    ]
+    for load in small + loads:
         load.start()
     for dy in range(1, 4):
         greet(barrier, 0, dy, 0, core)
@@ -62,14 +66,15 @@
         greet(barrier, s // 8, 0, s % 8, other)
         greet(barrier, s // 8, 0, s % 8, core)
 
-    m_buf[0] = mask[...]
+    for load in small:
+        load.wait()
 
     row_k = (iota((256, 16), 0) % 128) // 16 * 2 + iota((256, 16), 0) // 128
     pick_k = one_hot(row_k == iota((256, 16), 1))
-    by_level = jnp.dot(pick_k, vmodes[...], preferred_element_type=F32).astype(BF16)
+    by_level = jnp.dot(pick_k, v_buf[...], preferred_element_type=F32).astype(BF16)
     by_column = jnp.dot(by_level, one_hot(iota((20, 320), 1) // 16 == iota((20, 320), 0)), preferred_element_type=F32)
     owner_lane = jnp.dot(
-        owner[...].astype(F32).astype(BF16),
+        o_buf[...].astype(F32).astype(BF16),
         one_hot(iota((16, 320), 1) % 16 == iota((16, 320), 0)),
         preferred_element_type=F32,
     )
@@ -129,10 +134,10 @@
                     device_id=(to_slot * 2 + half, to_tm), device_id_type=MESH).start()
 
     mine = iota((256, 16), 0) % 16 == iota((256, 16), 1)
-    from_slot = jnp.sum(jnp.where(mine, owner[...].astype(F32), 0.0), axis=1, keepdims=True)
+    from_slot = jnp.sum(jnp.where(mine, o_buf[...].astype(F32), 0.0), axis=1, keepdims=True)
     row, column = iota((256, 256), 0), iota((256, 256), 1)
     order[...] = one_hot(((column // 16).astype(F32) == from_slot) & (column % 16 == row // 16))
-    give_order = pltpu.make_async_copy(order, order_out, o_sem)
+    give_order = pltpu.make_async_copy(order, order_out, i_sem.at[3])
     give_order.start()
 
     own_table.wait()
@@ -207,14 +212,16 @@
 
 
 def exchange(fields, vmodes, owner, table, mask):
-    vmem, hbm = pl.BlockSpec(memory_space=pltpu.VMEM), pl.BlockSpec(memory_space=pl.ANY)
+    hbm, free = pl.BlockSpec(memory_space=pltpu.HBM), pl.BlockSpec(memory_space=pl.ANY)
     dma = pltpu.SemaphoreType.DMA
     return pl.pallas_call(
         exchange_kernel,
         out_shape=[jax.ShapeDtypeStruct((256, 16, 128), BF16), jax.ShapeDtypeStruct((256, 256), BF16)],
-        in_specs=[hbm, vmem, vmem, hbm, vmem],
-        out_specs=[hbm, hbm],
+        in_specs=[hbm] * 5,
+        out_specs=[free, free],
         scratch_shapes=[
+            pltpu.VMEM((16, 20), BF16),
+            pltpu.VMEM((1, 16), jnp.int32),
             pltpu.VMEM((256, 256), BF16),
             pltpu.VMEM((3, 20, 20, 16, 32), BF16),
             pltpu.VMEM((320, 1920), BF16),
@@ -229,12 +236,12 @@
             pltpu.VMEM((960, 256), F32),
             pltpu.VMEM((960, 256), BF16),
             pltpu.VMEM((256, 16, 128), BF16),
-            dma, dma((3,)), dma((3,)), dma((2,)), dma, dma((4,)), dma, dma,
+            dma((4,)), dma((3,)), dma((3,)), dma((2,)), dma, dma((4,)), dma, dma,
             pltpu.SemaphoreType.REGULAR,
         ],
         compiler_params=pltpu.CompilerParams(collective_id=0, has_side_effects=True, vmem_limit_bytes=50 * 2**20),
         name="exchange",
-    )(fields, vmodes, owner, table, mask)
+    )(*(pltpu.with_memory_space_constraint(ref, pltpu.HBM) for ref in (fields, vmodes, owner, table, mask)))
 
 
 def layout_kernel(order, arrived, out, laid, sem):

time: 64.8 us -> 62.9 us (0.971)
  local copies, waits for them, and re-layouts: 2.03 us -> 0 us
    unnamed x6 -> x0, local copies, waits for them, and re-layouts: 2.03 us -> none
where the time goes in v4:
time: 62.9 us
  Pallas kernels  62.9 us (100%)
    pallas_call x1, Pallas kernels, exchange(): pl.pallas_call(exchange_kernel, out_shape=[jax.ShapeDtypeStruct((256, 16,...  60.4 us
    pallas_call x1, Pallas kernels, lay_out(): pl.pallas_call(layout_kernel, out_shape=jax.ShapeDtypeStruct((16, 3, 20,...  2.42 us

profile of v4, /device:TPU:1, one launch (start us, length us, event | category | flops | bytes accessed | tf_op | source)
XLA Modules:
  0.0 62.9 jit_solution(1283743978065858971)
XLA Ops:
  0.0 60.4 %exchange.1 = (bf16[256,16,128]{2,1,0:T(8,128)(2,1)S(1)}, bf16[256,256]{1,0:T(8,128)(2,1)S(1)}) custom-call(bf16[3,20,20,16,32]{4,3,2,1,0:T(8,128)(2,1)} %fields.1, bf16[16,20]{1,0:T(8,128)(2,1)} %bitcast.4, s32[1,16]{1,0:T(1,128)} %bitcast.5, bf16[2,480,1920]{2,1,0:T(8,128)(2,1)} %table.1, s32[2,480]{1,0:T(2,128)} %mask.1), custom_call_target="tpu_custom_call" | custom-call | tf_op jit(solution)/shard_map/exchange/pallas_call | solution.py:217
  60.4 2.4 %lay_out.1 = bf16[16,3,20,16,32]{4,3,2,1,0:T(8,128)(2,1)} custom-call(bf16[256,256]{1,0:T(8,128)(2,1)S(1)} %get-tuple-element.7.order, bf16[2,8,16,16,128]{4,3,2,1,0:T(8,128)(2,1)S(1)} %bitcast.3), custom_call_target="tpu_custom_call" | custom-call | tf_op jit(solution)/shard_map/lay_out/pallas_call | solution.py:267

commit v5 on v4

--- a/solution.py
+++ b/solution.py
@@ -35,8 +35,8 @@
 def exchange_kernel(
     fields, vmodes, owner, table, mask,
     arrived, order_out,
-    v_buf, o_buf, order, f_buf, f_cat, spread, send1, cols, xmat, t_nat, t_ana, t_syn, m_buf, coef, kept, send2,
-    i_sem, f_sem, t_sem, m_sem, s1_sem, r1_sem, s2_sem, r2_sem, ready,
+    v_buf, o_buf, order, f_buf, f_cat, spread, send1, cols, xmat, t_nat, t_ana, t_syn, m_buf, coef, kept, send2, handed,
+    i_sem, f_sem, t_sem, m_sem, s1_sem, r1_sem, s2_sem, r2_sem, x_sem, h_sem, ready,
 ):
     x, y, z, core = position()
     slot, tm = y * 4 + z % 4, x * 2 + z // 4
@@ -94,15 +94,16 @@
         src_ref=m_buf.at[0], dst_ref=m_buf.at[1], send_sem=m_sem.at[0], recv_sem=m_sem.at[1],
         device_id=partner, device_id_type=MESH)
     own_table = pltpu.make_async_copy(table.at[core], t_nat.at[pl.ds(0, 480)], t_sem.at[0])
-    spread[pl.ds(15, 128, stride=16), :] = jnp.zeros((128, 128), F32)
     my_place = y * 64 + tm * 8 + (z % 4) * 2 + core
 
     for half in range(2):
+        if half == 0:
+            spread[pl.ds(15, 128, stride=16), :] = jnp.dot(left[128:256], f_cat[:, 1792:1920], preferred_element_type=F32)
         for v in range(3):
             part = jnp.dot(left[half * 128:half * 128 + 128], f_cat[:, v * 640:v * 640 + 640], preferred_element_type=F32)
             for a in range(5):
                 spread[pl.ds(v * 5 + a, 128, stride=16), :] = part[:, a * 128:a * 128 + 128]
-        send1[pl.ds(half * 128, 128)] = spread[...].astype(BF16).reshape(128, 16, 128)
+        send1[pl.ds(half * 128, 128)] = spread[...].astype(BF16).reshape(128, 8, 2, 128)
         if half == 0:
             pl.semaphore_wait(barrier, 66)
             for dy in range(1, 4):
@@ -110,7 +111,8 @@
             other_mask.start()
             other_table.start()
             own_table.start()
-        stay = send1.at[half * 128 + tm * 16 + slot], cols.at[my_place]
+        pairs = pl.ds(0, 8 - half)
+        stay = send1.at[half * 128 + tm * 16 + slot, pairs], cols.at[my_place, pairs]
 
         @pl.when(core == half)
         def _():
@@ -119,7 +121,7 @@
         @pl.when(core != half)
         def _():
             pltpu.make_async_remote_copy(
-                *stay, send_sem=s1_sem, recv_sem=r1_sem.at[0], device_id=partner, device_id_type=MESH).start()
+                *stay, send_sem=s1_sem.at[half], recv_sem=r1_sem.at[0], device_id=partner, device_id_type=MESH).start()
 
         for dy in range(4):
             if half == 0 and dy == 1:
@@ -129,8 +131,8 @@
             def _(s):
                 to_slot, to_tm = shifted(x, y, z, s // 8, dy, s % 8)
                 pltpu.make_async_remote_copy(
-                    src_ref=send1.at[half * 128 + to_tm * 16 + to_slot], dst_ref=cols.at[my_place],
-                    send_sem=s1_sem, recv_sem=r1_sem.at[dy],
+                    src_ref=send1.at[half * 128 + to_tm * 16 + to_slot, pairs], dst_ref=cols.at[my_place, pairs],
+                    send_sem=s1_sem.at[half], recv_sem=r1_sem.at[dy],
                     device_id=(to_slot * 2 + half, to_tm), device_id_type=MESH).start()
 
     mine = iota((256, 16), 0) % 16 == iota((256, 16), 1)
@@ -151,16 +153,18 @@
         base = pl.multiple_of(g * 128, 128)
         def target(q):
             return g * 32 + (q // 16) % 8 * 20 + q // 128
+        def row_of(q):
+            return jnp.where(q % 16 < 14, q % 16, jnp.where(q % 16 == 14 + core, 14, -1))
         ana = jnp.zeros((960, 512), F32)
         syn = jnp.zeros((512, 960), F32)
         for v in range(3):
             window = t_nat[:, pl.ds(pl.multiple_of(v * 640 + base, 128), 256)]
             q, w = iota((256, 512), 1), iota((256, 512), 0)
-            r = q % 16 - v * 5
+            r = row_of(q) - v * 5
             hot = one_hot((w == target(q) + r * 4) & (r >= 0) & (r < 5))
             ana += jnp.dot(window, hot, preferred_element_type=F32)
             q, w = iota((512, 256), 0), iota((512, 256), 1)
-            r = q % 16 - v * 5
+            r = row_of(q) - v * 5
             hot = one_hot((w == target(q) + r * 4) & (r >= 0) & (r < 5))
             syn += lax.dot_general(hot, window, (((1,), (1,)), ((), ())), preferred_element_type=F32)
         part = pl.ds(pl.multiple_of(g * 512, 512), 512)
@@ -169,10 +173,25 @@
 
     for dy in range(4):
         g = (y + 4 - dy) % 4
-        landed = cols.at[pl.ds(g * 64, 64)]
-        pltpu.make_async_copy(landed, landed, r1_sem.at[dy]).wait()
+        block = pl.ds(g * 64, 64)
+        lent = pltpu.make_async_remote_copy(
+            src_ref=cols.at[block, 7], dst_ref=cols.at[block, 7], send_sem=x_sem.at[dy], recv_sem=x_sem.at[4 + dy],
+            device_id=partner, device_id_type=MESH)
+
+        @pl.when(core == 0)
+        def _():
+            pltpu.make_async_copy(cols.at[block], cols.at[block], r1_sem.at[dy]).wait()
+            lent.start()
+
+        @pl.when(core == 1)
+        def _():
+            first = cols.at[block, pl.ds(0, 7)]
+            pltpu.make_async_copy(first, first, r1_sem.at[dy]).wait()
+            lent.wait_recv()
+
+        tiles = [cols[pl.ds(g * 64 + t * 8, 8)].reshape(128, 128) for t in range(8)]
         for a in range(4):
-            pieces = [cols[pl.ds(g * 64 + t * 8, 8), :, a * 32:a * 32 + 32].reshape(128, 32) for t in range(8)]
+            pieces = [tile[:, a * 32:a * 32 + 32] for tile in tiles]
             xmat[a * 128:a * 128 + 128, :] = jnp.concatenate(pieces, axis=1)
         add = jnp.dot(t_ana[:, pl.ds(pl.multiple_of(g * 512, 512), 512)], xmat[...], preferred_element_type=F32)
         if dy == 0:
@@ -187,28 +206,63 @@
         back = jnp.dot(t_syn[pl.ds(pl.multiple_of(g * 512, 512), 512), :], kept[...], preferred_element_type=F32).astype(BF16)
         for t in range(8):
             pieces = [back[a * 128:a * 128 + 128, t * 32:t * 32 + 32] for a in range(4)]
-            send2[pl.ds(g * 64 + t * 8, 8)] = jnp.concatenate(pieces, axis=1).reshape(8, 16, 128)
-        home = arrived.at[core * 128 + tm * 16 + slot]
-        if dy == 0:
-            pltpu.make_async_copy(send2.at[my_place], home, r2_sem).start()
-            pltpu.make_async_remote_copy(
-                send2.at[y * 64 + tm * 8 + (z % 4) * 2 + other], home,
-                send_sem=s2_sem, recv_sem=r2_sem, device_id=partner, device_id_type=MESH).start()
-
-        @pl.loop(0 if dy else 1, 32)
-        def _(s):
-            to_slot, to_tm = shifted(x, y, z, s // 8, dy, s % 8)
-            for to_core in range(2):
+            send2[pl.ds(g * 64 + t * 8, 8)] = jnp.concatenate(pieces, axis=1).reshape(8, 8, 2, 128)
+        block = pl.ds(g * 64, 64)
+        hand = pltpu.make_async_remote_copy(
+            src_ref=send2.at[block, 7], dst_ref=handed.at[block], send_sem=h_sem.at[dy], recv_sem=h_sem.at[4 + dy],
+            device_id=partner, device_id_type=MESH)
+
+        def give_back(my_core):
+            pairs = pl.ds(0, 7 + my_core)
+            home = arrived.at[my_core * 128 + tm * 16 + slot, pairs]
+            if dy == 0:
+                pltpu.make_async_copy(send2.at[my_place, pairs], home, r2_sem.at[my_core]).start()
                 pltpu.make_async_remote_copy(
-                    src_ref=send2.at[g * 64 + to_tm * 8 + to_slot % 4 * 2 + to_core], dst_ref=home,
-                    send_sem=s2_sem, recv_sem=r2_sem,
-                    device_id=(to_slot * 2 + to_core, to_tm), device_id_type=MESH).start()
+                    send2.at[y * 64 + tm * 8 + (z % 4) * 2 + 1 - my_core, pairs], home,
+                    send_sem=s2_sem, recv_sem=r2_sem.at[my_core], device_id=partner, device_id_type=MESH).start()
+
+            @pl.loop(0 if dy else 1, 32)
+            def _(s):
+                to_slot, to_tm = shifted(x, y, z, s // 8, dy, s % 8)
+                for to_core in range(2):
+                    pltpu.make_async_remote_copy(
+                        src_ref=send2.at[g * 64 + to_tm * 8 + to_slot % 4 * 2 + to_core, pairs], dst_ref=home,
+                        send_sem=s2_sem, recv_sem=r2_sem.at[my_core],
+                        device_id=(to_slot * 2 + to_core, to_tm), device_id_type=MESH).start()
+
+        @pl.when(core == 0)
+        def _():
+            hand.start()
+            give_back(0)
+
+        @pl.when(core == 1)
+        def _():
+            hand.wait_recv()
+            send2[block, 7] = send2[block, 7] + handed[block]
+            give_back(1)
 
     give_order.wait()
-    sent = pl.ds(0, 255)
-    pltpu.make_async_copy(send1.at[sent], send1.at[sent], s1_sem).wait()
-    pltpu.make_async_copy(send2.at[sent], send2.at[sent], s2_sem).wait()
-    pltpu.make_async_copy(arrived, arrived, r2_sem).wait()
+
+    def settle(ref, sem):
+        pltpu.make_async_copy(ref, ref, sem).wait()
+
+    @pl.when(core == 0)
+    def _():
+        settle(send1.at[pl.ds(0, 127)], s1_sem.at[0])
+        settle(send1.at[pl.ds(0, 128), pl.ds(0, 7)], s1_sem.at[1])
+        settle(send2.at[pl.ds(0, 255), pl.ds(0, 7)], s2_sem)
+        for dy in range(4):
+            settle(handed.at[pl.ds(0, 64)], x_sem.at[dy])
+            settle(handed.at[pl.ds(0, 64)], h_sem.at[dy])
+
+    @pl.when(core == 1)
+    def _():
+        settle(send1.at[pl.ds(0, 128)], s1_sem.at[0])
+        settle(send1.at[pl.ds(0, 127), pl.ds(0, 7)], s1_sem.at[1])
+        settle(send2.at[pl.ds(0, 255)], s2_sem)
+
+    settle(arrived.at[pl.ds(0, 128), pl.ds(0, 7)], r2_sem.at[0])
+    settle(arrived.at[pl.ds(128, 128)], r2_sem.at[1])
 
 
 def exchange(fields, vmodes, owner, table, mask):
@@ -216,7 +270,7 @@
     dma = pltpu.SemaphoreType.DMA
     return pl.pallas_call(
         exchange_kernel,
-        out_shape=[jax.ShapeDtypeStruct((256, 16, 128), BF16), jax.ShapeDtypeStruct((256, 256), BF16)],
+        out_shape=[jax.ShapeDtypeStruct((256, 8, 2, 128), BF16), jax.ShapeDtypeStruct((256, 256), BF16)],
         in_specs=[hbm] * 5,
         out_specs=[free, free],
         scratch_shapes=[
@@ -226,8 +280,8 @@
             pltpu.VMEM((3, 20, 20, 16, 32), BF16),
             pltpu.VMEM((320, 1920), BF16),
             pltpu.VMEM((2048, 128), F32),
-            pltpu.VMEM((256, 16, 128), BF16),
-            pltpu.VMEM((256, 16, 128), BF16),
+            pltpu.VMEM((256, 8, 2, 128), BF16),
+            pltpu.VMEM((256, 8, 2, 128), BF16),
             pltpu.VMEM((512, 256), BF16),
             pltpu.VMEM((960, 1920), BF16),
             pltpu.VMEM((960, 2048), BF16),
@@ -235,8 +289,9 @@
             pltpu.VMEM((2, 2, 480), jnp.int32),
             pltpu.VMEM((960, 256), F32),
             pltpu.VMEM((960, 256), BF16),
-            pltpu.VMEM((256, 16, 128), BF16),
-            dma((4,)), dma((3,)), dma((3,)), dma((2,)), dma, dma((4,)), dma, dma,
+            pltpu.VMEM((256, 8, 2, 128), BF16),
+            pltpu.VMEM((256, 2, 128), BF16),
+            dma((4,)), dma((3,)), dma((3,)), dma((2,)), dma((2,)), dma((4,)), dma, dma((2,)), dma((8,)), dma((8,)),
             pltpu.SemaphoreType.REGULAR,
         ],
         compiler_params=pltpu.CompilerParams(collective_id=0, has_side_effects=True, vmem_limit_bytes=50 * 2**20),
@@ -247,14 +302,18 @@
 def layout_kernel(order, arrived, out, laid, sem):
     copies = []
     for t in range(8):
-        tiles = [arrived[core, t].reshape(256, 128) for core in range(2)]
-        rows = jnp.dot(order[...], jnp.concatenate(tiles, axis=1), preferred_element_type=F32)
+        first = jnp.where(iota((256, 128), 0) % 16 < 14, arrived[0, t].reshape(256, 128).astype(F32), 0.0).astype(BF16)
+        both = jnp.concatenate([first, arrived[1, t].reshape(256, 128)], axis=1)
+        rows = jnp.dot(order[...], both, preferred_element_type=F32)
         for core in range(2):
             for a in range(4):
                 part = rows[:, core * 128:core * 128 + 128]
                 part = (pltpu.roll(part, 128 - a * 32, 1) if a else part).astype(BF16)
-                for r in range(15):
+                for r in range(14):
                     laid[t * 2 + core, r // 5, r % 5 * 4 + a] = part[r * 16:r * 16 + 16, 0:32]
+                if core == 1:
+                    laid[t * 2, 2, 16 + a] = part[224:240, 0:32]
+                    laid[t * 2 + 1, 2, 16 + a] = part[240:256, 0:32]
         span = pl.ds(t * 2, 2)
         copies.append(pltpu.make_async_copy(laid.at[span], out.at[span], sem.at[t]))
         copies[-1].start()

time: 62.9 us -> 60.7 us (0.965)
  Pallas kernels: 62.9 us -> 60.6 us
    pallas_call x1, Pallas kernels: 60.4 us -> 58.2 us  [exchange(): pl.pallas_call(exchange_kernel, out_shape=[jax.ShapeDtypeStruct((256, 8,...]
where the time goes in v5:
time: 60.7 us; the launch traced here: 60.6 us
  Pallas kernels  60.6 us (100%)
    pallas_call x1, Pallas kernels, exchange(): pl.pallas_call(exchange_kernel, out_shape=[jax.ShapeDtypeStruct((256, 8,...  58.2 us
    pallas_call x1, Pallas kernels, lay_out(): pl.pallas_call(layout_kernel, out_shape=jax.ShapeDtypeStruct((16, 3, 20,...  2.44 us

profile of v5, /device:TPU:1, one launch (start us, length us, event | category | flops | bytes accessed | tf_op | source)
XLA Modules:
  0.0 60.6 jit_solution(16060286043379507521)
XLA Ops:
  0.0 58.2 %exchange.1 = (bf16[256,8,2,128]{3,2,1,0:T(2,128)(2,1)S(1)}, bf16[256,256]{1,0:T(8,128)(2,1)S(1)}) custom-call(bf16[3,20,20,16,32]{4,3,2,1,0:T(8,128)(2,1)} %fields.1, bf16[16,20]{1,0:T(8,128)(2,1)} %bitcast.4, s32[1,16]{1,0:T(1,128)} %bitcast.5, bf16[2,480,1920]{2,1,0:T(8,128)(2,1)} %table.1, s32[2,480]{1,0:T(2,128)} %mask.1), custom_call_target="tpu_custom_call" | custom-call | tf_op jit(solution)/shard_map/exchange/pallas_call | solution.py:271
  58.2 2.4 %lay_out.1 = bf16[16,3,20,16,32]{4,3,2,1,0:T(8,128)(2,1)} custom-call(bf16[256,256]{1,0:T(8,128)(2,1)S(1)} %get-tuple-element.7.order, bf16[2,8,16,16,128]{4,3,2,1,0:T(8,128)(2,1)S(1)} %bitcast.3), custom_call_target="tpu_custom_call" | custom-call | tf_op jit(solution)/shard_map/lay_out/pallas_call | solution.py:326

commit v6 on v5

--- a/solution.py
+++ b/solution.py
@@ -25,11 +25,6 @@
     core, z_lo, y = lat % 2, (lat // 2) % 4, lat // 8
     x, z_hi = tm // 2, tm % 2
     return x, y, z_hi * 4 + z_lo, core
-
-
-def shifted(x, y, z, dx, dy, dz):
-    x, y, z = (x + dx) % 4, (y + dy) % 4, (z + dz) % 8
-    return y * 4 + z % 4, x * 2 + z // 4
 
 
 def exchange_kernel(
@@ -40,15 +35,29 @@
 ):
     x, y, z, core = position()
     slot, tm = y * 4 + z % 4, x * 2 + z // 4
+    by_x = [(x + dx) % 4 * 2 for dx in range(4)]
+    by_y = [(y + dy) % 4 * 4 for dy in range(4)]
+    by_z = [((z + dz) % 8 % 4, (z + dz) % 8 // 4) for dz in range(8)]
+
+    def each_chip(dy, visit):
+        if dy == 0:
+            for low, high in by_z[1:]:
+                visit(by_y[0] + low, by_x[0] + high)
+
+        @pl.loop(0 if dy else 1, 4)
+        def _(dx):
+            along_x = (x + dx) % 4 * 2
+            for low, high in by_z:
+                visit(by_y[dy] + low, along_x + high)
+
     lat = slot * 2 + core
     other = 1 - core
     partner = (slot * 2 + other, tm)
 
     barrier = pltpu.get_barrier_semaphore()
 
-    def greet(sem, dx, dy, dz, to_core):
-        s, t = shifted(x, y, z, dx, dy, dz)
-        pl.semaphore_signal(sem, inc=1, device_id=(s * 2 + to_core, t), device_id_type=MESH)
+    def greet(sem, to_slot, to_tm, to_core):
+        pl.semaphore_signal(sem, inc=1, device_id=(to_slot * 2 + to_core, to_tm), device_id_type=MESH)
 
     loads = [pltpu.make_async_copy(fields.at[v], f_buf.at[v], f_sem.at[v]) for v in range(3)]
     small = [
@@ -57,14 +66,13 @@
     ]
     for load in small + loads:
         load.start()
+    for dx in range(4):
+        for dz, (low, high) in enumerate(by_z):
+            greet(barrier, by_y[0] + low, by_x[dx] + high, other)
+            if dx or dz:
+                greet(barrier, by_y[0] + low, by_x[dx] + high, core)
     for dy in range(1, 4):
-        greet(barrier, 0, dy, 0, core)
-    greet(barrier, 0, 0, 0, other)
-
-    @pl.loop(1, 32)
-    def _(s):
-        greet(barrier, s // 8, 0, s % 8, other)
-        greet(barrier, s // 8, 0, s % 8, core)
+        greet(barrier, by_y[dy] + by_z[0][0], tm, core)
 
     for load in small:
         load.wait()
@@ -107,7 +115,7 @@
         if half == 0:
             pl.semaphore_wait(barrier, 66)
             for dy in range(1, 4):
-                greet(ready, 0, dy, 0, core)
+                greet(ready, by_y[dy] + by_z[0][0], tm, core)
             other_mask.start()
             other_table.start()
             own_table.start()
@@ -127,13 +135,13 @@
             if half == 0 and dy == 1:
                 pl.semaphore_wait(ready, 3)
 
-            @pl.loop(0 if dy else 1, 32)
-            def _(s):
-                to_slot, to_tm = shifted(x, y, z, s // 8, dy, s % 8)
+            def send(to_slot, to_tm):
                 pltpu.make_async_remote_copy(
                     src_ref=send1.at[half * 128 + to_tm * 16 + to_slot, pairs], dst_ref=cols.at[my_place, pairs],
                     send_sem=s1_sem.at[half], recv_sem=r1_sem.at[dy],
                     device_id=(to_slot * 2 + half, to_tm), device_id_type=MESH).start()
+
+            each_chip(dy, send)
 
     mine = iota((256, 16), 0) % 16 == iota((256, 16), 1)
     from_slot = jnp.sum(jnp.where(mine, o_buf[...].astype(F32), 0.0), axis=1, keepdims=True)
@@ -221,14 +229,14 @@
                     send2.at[y * 64 + tm * 8 + (z % 4) * 2 + 1 - my_core, pairs], home,
                     send_sem=s2_sem, recv_sem=r2_sem.at[my_core], device_id=partner, device_id_type=MESH).start()
 
-            @pl.loop(0 if dy else 1, 32)
-            def _(s):
-                to_slot, to_tm = shifted(x, y, z, s // 8, dy, s % 8)
+            def send(to_slot, to_tm):
                 for to_core in range(2):
                     pltpu.make_async_remote_copy(
                         src_ref=send2.at[g * 64 + to_tm * 8 + to_slot % 4 * 2 + to_core, pairs], dst_ref=home,
                         send_sem=s2_sem, recv_sem=r2_sem.at[my_core],
                         device_id=(to_slot * 2 + to_core, to_tm), device_id_type=MESH).start()
+
+            each_chip(dy, send)
 
         @pl.when(core == 0)
         def _():

time: 60.7 us -> 59.8 us (0.985)
  Pallas kernels: 60.6 us -> 59.7 us
    pallas_call x1, Pallas kernels: 58.2 us -> 57.3 us  [exchange(): pl.pallas_call(exchange_kernel, out_shape=[jax.ShapeDtypeStruct((256, 8,...]
where the time goes in v6:
time: 59.8 us; the launch traced here: 59.7 us
  Pallas kernels  59.7 us (100%)
    pallas_call x1, Pallas kernels, exchange(): pl.pallas_call(exchange_kernel, out_shape=[jax.ShapeDtypeStruct((256, 8,...  57.3 us
    pallas_call x1, Pallas kernels, lay_out(): pl.pallas_call(layout_kernel, out_shape=jax.ShapeDtypeStruct((16, 3, 20,...  2.44 us

profile of v6, /device:TPU:1, one launch (start us, length us, event | category | flops | bytes accessed | tf_op | source)
XLA Modules:
  0.0 59.7 jit_solution(10413685316124435593)
XLA Ops:
  0.0 57.3 %exchange.1 = (bf16[256,8,2,128]{3,2,1,0:T(2,128)(2,1)S(1)}, bf16[256,256]{1,0:T(8,128)(2,1)S(1)}) custom-call(bf16[3,20,20,16,32]{4,3,2,1,0:T(8,128)(2,1)} %fields.1, bf16[16,20]{1,0:T(8,128)(2,1)} %bitcast.4, s32[1,16]{1,0:T(1,128)} %bitcast.5, bf16[2,480,1920]{2,1,0:T(8,128)(2,1)} %table.1, s32[2,480]{1,0:T(2,128)} %mask.1), custom_call_target="tpu_custom_call" | custom-call | tf_op jit(solution)/shard_map/exchange/pallas_call | solution.py:279
  57.3 2.4 %lay_out.1 = bf16[16,3,20,16,32]{4,3,2,1,0:T(8,128)(2,1)} custom-call(bf16[256,256]{1,0:T(8,128)(2,1)S(1)} %get-tuple-element.7.order, bf16[2,8,16,16,128]{4,3,2,1,0:T(8,128)(2,1)S(1)} %bitcast.3), custom_call_target="tpu_custom_call" | custom-call | tf_op jit(solution)/shard_map/lay_out/pallas_call | solution.py:334

commit v7 on v6

--- a/solution.py
+++ b/solution.py
@@ -209,7 +209,7 @@
         else:
             kept[...] = (coef[...] + add).astype(BF16)
 
-    for dy in range(4):
+    for dy in (2, 1, 3, 0):
         g = (y + dy) % 4
         back = jnp.dot(t_syn[pl.ds(pl.multiple_of(g * 512, 512), 512), :], kept[...], preferred_element_type=F32).astype(BF16)
         for t in range(8):

time: 59.8 us -> 59.4 us (level)
  no operation moved by 1% of the time
where the time goes in v7:
time: 59.4 us; the launch traced here: 59.3 us
  Pallas kernels  59.3 us (100%)
    pallas_call x1, Pallas kernels, exchange(): pl.pallas_call(exchange_kernel, out_shape=[jax.ShapeDtypeStruct((256, 8,...  56.8 us
    pallas_call x1, Pallas kernels, lay_out(): pl.pallas_call(layout_kernel, out_shape=jax.ShapeDtypeStruct((16, 3, 20,...  2.44 us

profile of v7, /device:TPU:1, one launch (start us, length us, event | category | flops | bytes accessed | tf_op | source)
XLA Modules:
  0.0 59.3 jit_solution(3242949916698643161)
XLA Ops:
  0.0 56.8 %exchange.1 = (bf16[256,8,2,128]{3,2,1,0:T(2,128)(2,1)S(1)}, bf16[256,256]{1,0:T(8,128)(2,1)S(1)}) custom-call(bf16[3,20,20,16,32]{4,3,2,1,0:T(8,128)(2,1)} %fields.1, bf16[16,20]{1,0:T(8,128)(2,1)} %bitcast.4, s32[1,16]{1,0:T(1,128)} %bitcast.5, bf16[2,480,1920]{2,1,0:T(8,128)(2,1)} %table.1, s32[2,480]{1,0:T(2,128)} %mask.1), custom_call_target="tpu_custom_call" | custom-call | tf_op jit(solution)/shard_map/exchange/pallas_call | solution.py:279
  56.8 2.4 %lay_out.1 = bf16[16,3,20,16,32]{4,3,2,1,0:T(8,128)(2,1)} custom-call(bf16[256,256]{1,0:T(8,128)(2,1)S(1)} %get-tuple-element.7.order, bf16[2,8,16,16,128]{4,3,2,1,0:T(8,128)(2,1)S(1)} %bitcast.3), custom_call_target="tpu_custom_call" | custom-call | tf_op jit(solution)/shard_map/lay_out/pallas_call | solution.py:334

commit v8 on v7

--- a/solution.py
+++ b/solution.py
@@ -41,14 +41,14 @@
 
     def each_chip(dy, visit):
         if dy == 0:
-            for low, high in by_z[1:]:
-                visit(by_y[0] + low, by_x[0] + high)
+            for dz in (4, 3, 5, 2, 6, 1, 7):
+                visit(by_y[0] + by_z[dz][0], by_x[0] + by_z[dz][1])
 
         @pl.loop(0 if dy else 1, 4)
         def _(dx):
             along_x = (x + dx) % 4 * 2
-            for low, high in by_z:
-                visit(by_y[dy] + low, along_x + high)
+            for dz in (4, 3, 5, 2, 6, 1, 7, 0):
+                visit(by_y[dy] + by_z[dz][0], along_x + by_z[dz][1])
 
     lat = slot * 2 + core
     other = 1 - core

time: 59.4 us -> 58.9 us (level)
  no operation moved by 1% of the time
where the time goes in v8:
time: 58.9 us; the launch traced here: 58.8 us
  Pallas kernels  58.8 us (100%)
    pallas_call x1, Pallas kernels, exchange(): pl.pallas_call(exchange_kernel, out_shape=[jax.ShapeDtypeStruct((256, 8,...  56.4 us
    pallas_call x1, Pallas kernels, lay_out(): pl.pallas_call(layout_kernel, out_shape=jax.ShapeDtypeStruct((16, 3, 20,...  2.44 us

profile of v8, /device:TPU:1, one launch (start us, length us, event | category | flops | bytes accessed | tf_op | source)
XLA Modules:
  0.0 58.8 jit_solution(15453329225923048605)
XLA Ops:
  0.0 56.4 %exchange.1 = (bf16[256,8,2,128]{3,2,1,0:T(2,128)(2,1)S(1)}, bf16[256,256]{1,0:T(8,128)(2,1)S(1)}) custom-call(bf16[3,20,20,16,32]{4,3,2,1,0:T(8,128)(2,1)} %fields.1, bf16[16,20]{1,0:T(8,128)(2,1)} %bitcast.4, s32[1,16]{1,0:T(1,128)} %bitcast.5, bf16[2,480,1920]{2,1,0:T(8,128)(2,1)} %table.1, s32[2,480]{1,0:T(2,128)} %mask.1), custom_call_target="tpu_custom_call" | custom-call | tf_op jit(solution)/shard_map/exchange/pallas_call | solution.py:279
  56.4 2.4 %lay_out.1 = bf16[16,3,20,16,32]{4,3,2,1,0:T(8,128)(2,1)} custom-call(bf16[256,256]{1,0:T(8,128)(2,1)S(1)} %get-tuple-element.7.order, bf16[2,8,16,16,128]{4,3,2,1,0:T(8,128)(2,1)S(1)} %bitcast.3), custom_call_target="tpu_custom_call" | custom-call | tf_op jit(solution)/shard_map/lay_out/pallas_call | solution.py:334
